TPU v7x, 32 devices: a whole 2x2x4 slice. The times are simulated.
32 devices in a mesh: row: 8 (over z, y), col: 4 (over x, core).
Axes of the slice: x: 2, y: 2, z: 4, core: 2. Of those that a mesh axis runs over, the one named last changes fastest.
Arguments:
- interaction: bfloat16 [8192, 8192], P('row', 'col'), may hold values from -0.0625 to 0.0625
- amplitudes: bfloat16 [8192, 8192], P('row', 'col'), may hold values from -6 to 6
- driver: bfloat16 [8192, 8192], P('row', 'col'), may hold values from -6 to 6
- dressing: bfloat16 [1024, 1024], replicated, may hold values from -0.1875 to 0.1875
- occ_energy: float32 [8], replicated, may hold values from -2 to -0.5
- vir_energy: float32 [1024], replicated, may hold values from 0.5 to 3
Outputs:
- updated: float32 [8192, 8192], P('row', 'col')
All inputs are finite; a program needn't handle non-finite values.
Results may differ from a plain program's by a relative error of at most 0.00084.
Values may be sent and summed in bfloat16 or wider, within the bound.
A program may use at most 128 MiB of HBM per device.

v0:
```python
import functools

import jax
import jax.numpy as jnp
from jax import lax
from jax.experimental import pallas as pl
from jax.experimental.pallas import tpu as pltpu
from jax.sharding import PartitionSpec as P


def ring_owner(position, count):
    return jnp.where(position < count // 2, 2 * position, 2 * (count - 1 - position) + 1)


def ring_position(index, count):
    return jnp.where(index % 2 == 0, index // 2, count - 1 - index // 2)


def line_energy(occupied, virtual, offset, length):
    orbitals = virtual.shape[0]
    energy = jnp.repeat(occupied, orbitals) - jnp.tile(virtual, occupied.shape[0])
    return lax.dynamic_slice_in_dim(energy, offset, length)


def dress(first_order, dressing):
    orbitals = dressing.shape[0]
    rows, columns = first_order.shape
    if columns % orbitals == 0:
        parts = [
            jnp.dot(first_order[:, j : j + orbitals], dressing, preferred_element_type=jnp.float32).astype(jnp.bfloat16)
            for j in range(0, columns, orbitals)
        ]
        return jnp.concatenate(parts, axis=1)
    lines = lax.all_to_all(first_order, "col", split_axis=0, concat_axis=1, tiled=True)
    line_rows, line_columns = lines.shape
    flattened = lines.reshape(line_rows * (line_columns // orbitals), orbitals)
    dressed_lines = jnp.dot(flattened, dressing, preferred_element_type=jnp.float32)
    dressed_lines = dressed_lines.reshape(line_rows, line_columns).astype(jnp.bfloat16)
    return lax.all_to_all(dressed_lines, "col", split_axis=1, concat_axis=0, tiled=True)


def cycle(interaction, amplitudes, count):
    order = list(range(0, count, 2)) + list(range(count - 1, 0, -2))
    up = [(order[p], order[(p + 1) % count]) for p in range(count)]
    down = [(b, a) for a, b in up]
    panel = lax.all_gather(interaction, "col", axis=1, tiled=True)
    depth = amplitudes.shape[0]
    half = depth // 2
    place = ring_position(lax.axis_index("row"), count)
    total = None
    waiting = []
    high, low = amplitudes[:half], amplitudes[half:]
    for step in range(count):
        if step < count - 1:
            next_high = lax.ppermute(high, "row", up)
            next_low = lax.ppermute(low, "row", down)
        waiting += [(high, place - step, 0), (low, place + step, half)]
        for block, position, shift in waiting if step >= 2 else ():
            owner = ring_owner((position + count) % count, count)
            part = lax.dynamic_slice_in_dim(panel, owner * depth + shift, half, axis=1)
            term = jnp.dot(part, block, preferred_element_type=jnp.float32)
            total = term if total is None else total + term
        if step >= 2:
            waiting = []
            next_high, next_low, total = lax.optimization_barrier((next_high, next_low, total))
        else:
            next_high, next_low = lax.optimization_barrier((next_high, next_low))
        high, low = next_high, next_low
    return total


MESH = pl.DeviceIdType.MESH
SUBS = 4


def ring_kernel(
    count, cols, lines, amplitudes, interaction, driver, dressing, row_energy, column_energy, out,
    land, panel, total, driver_line, operator, send_sem, recv_sem, w_send, w_recv, own_sem, local_sem,
):
    row, col = lax.axis_index("row"), lax.axis_index("col")
    place = jnp.where(lax.rem(row, 2) == 0, lax.div(row, 2), count - 1 - lax.div(row, 2))
    up = ring_owner(lax.rem(place + 1, count), count)
    down = ring_owner(lax.rem(place + count - 1, count), count)
    sibling = col + 1 - 2 * lax.rem(col, 2)
    half, width = land.shape[2], land.shape[3]
    depth = 2 * half
    per = panel.shape[2] // depth
    orbitals = operator.shape[0]
    group = count * SUBS
    slots = lines * group
    chips = cols // 2
    events = slots - lines * SUBS
    start = events - slots // 2

    barrier = pltpu.get_barrier_semaphore()
    partners = [(up, col), (down, col), (row, sibling)]
    partners += [(row, lax.rem(col + 2 * k, cols)) for k in range(1, chips)]
    for partner in partners:
        pl.semaphore_signal(barrier, inc=1, device_id=partner, device_id_type=MESH)
    pl.semaphore_wait(barrier, len(partners))

    def hop(way, source, slot):
        return pltpu.make_async_remote_copy(
            src_ref=source, dst_ref=land.at[way, slot], send_sem=send_sem.at[way, slot],
            recv_sem=recv_sem.at[way, slot], device_id=((up, down)[way], col), device_id_type=MESH,
        )

    def own_block(way, line, sub):
        return amplitudes.at[pl.ds(way * half, half), pl.ds(line * orbitals + sub * width, width)]

    for sub in range(SUBS):
        for way in range(2):
            hop(way, own_block(way, 0, sub), SUBS + sub).start()

    def w_copy(index, source, slot, target):
        return pltpu.make_async_remote_copy(
            src_ref=source, dst_ref=panel.at[slot], send_sem=w_send.at[index],
            recv_sem=w_recv.at[index], device_id=(row, target), device_id_type=MESH,
        )

    def from_chip(k):
        return lax.rem(col + cols - 2 * k, cols)

    for k in range(1, chips):
        w_copy(2 * k - 1, interaction, col, lax.rem(col + 2 * k, cols)).start()
    w_copy(0, interaction, col, sibling).start()

    own_copies = [
        pltpu.make_async_copy(own_block(way, line, sub), land.at[way, line * group + sub], own_sem.at[way, line * SUBS + sub])
        for line in range(lines) for sub in range(SUBS) for way in range(2)
    ]
    own_copies.append(pltpu.make_async_copy(interaction, panel.at[col], local_sem.at[0]))
    own_copies.append(pltpu.make_async_copy(dressing, operator, local_sem.at[1]))
    for copy in own_copies:
        copy.start()

    def load_driver(line):
        return pltpu.make_async_copy(
            driver.at[:, pl.ds(pl.multiple_of(line * orbitals, orbitals), orbitals)], driver_line, local_sem.at[2]
        )

    def write_line(line):
        return pltpu.make_async_copy(
            total, out.at[:, pl.ds(pl.multiple_of(line * orbitals, orbitals), orbitals)], local_sem.at[3]
        )

    load_driver(0).start()
    for copy in own_copies:
        copy.wait()

    def begin_line(line):
        @pl.when(line > 0)
        def _():
            write_line(line - 1).wait()

        load_driver(line).wait()
        total[...] = driver_line[...].astype(jnp.float32)

        @pl.when(line + 1 < lines)
        def _():
            load_driver(line + 1).start()

    tile = total.shape[0] // 4

    def end_line(line):
        @pl.loop(0, 4)
        def _(index):
            rows = pl.ds(pl.multiple_of(index * tile, tile), tile)
            summed = total[rows, :]
            denominator = row_energy[rows, :] + column_energy[pl.ds(line, 1), :]
            first_order = (summed / denominator).astype(jnp.bfloat16)
            dressed = jnp.dot(first_order, operator[...], preferred_element_type=jnp.float32).astype(jnp.bfloat16)
            total[rows, :] = (summed + dressed.astype(jnp.float32)) / denominator

        write_line(line).start()

    def multiply(item):
        line, within = lax.div(item, group), lax.rem(item, group)
        step, sub = lax.div(within, SUBS), lax.rem(within, SUBS)

        @pl.when(within == 0)
        def _():
            begin_line(line)

        def term(way, position):
            owner = ring_owner(lax.rem(position + count, count), count)
            columns = pl.ds(pl.multiple_of(lax.rem(owner, per) * depth + way * half, half), half)
            return jnp.dot(
                panel[lax.div(owner, per), :, columns], land[way, item], preferred_element_type=jnp.float32
            )

        place_columns = pl.ds(pl.multiple_of(sub * width, width), width)
        total[:, place_columns] += term(0, place - step) + term(1, place + step)

        @pl.when(within == group - 1)
        def _():
            end_line(line)

    @pl.loop(0, events)
    def _(event):
        line = lax.div(event, group - SUBS)
        slot = event + SUBS * (line + 1)
        last = lax.rem(slot, group) >= group - SUBS
        source = jnp.where(last, slot + SUBS, slot)
        for way in range(2):
            hop(way, land.at[way, slot], slot).wait_recv()

            @pl.when(source + SUBS < slots)
            def _():
                hop(way, land.at[way, source], source + SUBS).start()

        @pl.when(event == start * 3 // 4)
        def _():
            for k in range(1, chips):
                origin = from_chip(k)
                w_copy(2 * k - 1, panel.at[origin], origin, sibling).wait_recv()
                w_copy(2 * k, panel.at[origin], origin, sibling).start()

        @pl.when(event == start)
        def _():
            w_copy(0, interaction, sibling, sibling).wait_recv()
            for k in range(1, chips):
                origin = lax.rem(sibling + cols - 2 * k, cols)
                w_copy(2 * k, panel.at[origin], origin, sibling).wait_recv()

        @pl.when(event >= start)
        def _():
            @pl.loop(0, 2)
            def _(which):
                multiply(2 * (event - start) + which)

    write_line(lines - 1).wait()

    @pl.loop(0, events)
    def _(event):
        slot = event + SUBS * (lax.div(event, group - SUBS) + 1)
        for way in range(2):
            hop(way, land.at[way, slot], slot).wait_send()

    w_copy(0, interaction, col, sibling).wait_send()
    for k in range(1, chips):
        w_copy(2 * k - 1, interaction, col, sibling).wait_send()
        origin = from_chip(k)
        w_copy(2 * k, panel.at[origin], origin, sibling).wait_send()


def whole_lines(mesh, interaction, amplitudes, driver, dressing, row_energy, column_energy):
    count, cols = mesh.shape["row"], mesh.shape["col"]
    rows, columns = driver.shape
    depth = amplitudes.shape[0]
    orbitals = dressing.shape[0]
    lines = columns // orbitals
    slots = lines * count * SUBS
    dma = pltpu.SemaphoreType.DMA
    anywhere = pl.BlockSpec(memory_space=pl.ANY)
    vmem = pl.BlockSpec(memory_space=pltpu.VMEM)
    return pl.pallas_call(
        functools.partial(ring_kernel, count, cols, lines),
        out_shape=jax.ShapeDtypeStruct((rows, columns), jnp.float32),
        in_specs=[anywhere] * 4 + [vmem] * 2,
        out_specs=anywhere,
        scratch_shapes=[
            pltpu.VMEM((2, slots, depth // 2, orbitals // SUBS), jnp.bfloat16),
            pltpu.VMEM((cols,) + interaction.shape, jnp.bfloat16),
            pltpu.VMEM((rows, orbitals), jnp.float32),
            pltpu.VMEM((rows, orbitals), jnp.bfloat16),
            pltpu.VMEM(dressing.shape, jnp.bfloat16),
            dma((2, slots)),
            dma((2, slots)),
            dma((cols - 1,)),
            dma((cols - 1,)),
            dma((2, lines * SUBS)),
            dma((4,)),
        ],
        compiler_params=pltpu.CompilerParams(
            collective_id=0, has_side_effects=True, vmem_limit_bytes=62 * 1024 * 1024
        ),
        cost_estimate=pl.CostEstimate(
            flops=2 * rows * columns * (depth * count + orbitals), bytes_accessed=2 * rows * columns * 10, transcendentals=0
        ),
    )(amplitudes, interaction, driver, dressing, row_energy[:, None], column_energy.reshape(lines, orbitals))


def solution(mesh):
    count = mesh.shape["row"]

    def on_device(interaction, amplitudes, driver, dressing, occ_energy, vir_energy):
        row_count, column_count = driver.shape
        row_energy = line_energy(occ_energy, vir_energy, lax.axis_index("row") * row_count, row_count)
        column_energy = line_energy(occ_energy, vir_energy, lax.axis_index("col") * column_count, column_count)
        if column_count % dressing.shape[0] == 0:
            return whole_lines(mesh, interaction, amplitudes, driver, dressing, row_energy, column_energy)
        cycle_term = cycle(interaction, amplitudes, count)
        denominator = row_energy[:, None] + column_energy[None, :]
        summed = driver.astype(jnp.float32) + cycle_term
        first_order = (summed / denominator).astype(jnp.bfloat16)
        dressed = dress(first_order, dressing)
        return (summed + dressed.astype(jnp.float32)) / denominator

    return jax.shard_map(
        on_device,
        mesh=mesh,
        in_specs=(P("row", "col"), P("row", "col"), P("row", "col"), P(), P(), P()),
        out_specs=P("row", "col"),
        check_vma=False,
    )
```

profile of v0, /device:TPU:0, one launch (start us, length us, event | category | flops | bytes accessed | tf_op | source)
XLA Modules:
  0.0 341.1 jit_solution(11100872306360847562)
XLA Ops:
  0.0 0.8 subtract_bitcast_fusion
  0.8 0.6 reshape.7.column_energy
  1.4 1.0 copy.7.row_energy
  2.4 330.7 %shard_map.64 = f32[1024,2048]{1,0:T(8,128)} custom-call(bf16[1024,2048]{1,0:T(8,128)(2,1)} %amplitudes.1, bf16[1024,2048]{1,0:T(8,128)(2,1)} %interaction.1, bf16[1024,2048]{1,0:T(8,128)(2,1)} %driver.1, bf16[1024,1024]{1,0:T(8,128)(2,1)} %dressing.1, f32[1024,1]{1,0:T(8,128)} %copy.7.row_energy, f32[2,1024]{1,0:T(2,128)} %reshape.7.column_energy), custom_call_target="tpu_custom_call" | custom-call | flops 38654705664 | bytes 41943040 | tf_op jit(solution)/shard_map/pallas_call | solution.py:257
  333.2 7.9 %copy.12 = f32[1024,2048]{1,0:T(8,128)} copy(f32[1024,2048]{1,0:T(8,128)} %shard_map.64) | data formatting | bytes 16777216
  (3 shorter events, 0.0 us)
where the time goes:
time: 341 us
  Pallas kernels  331 us (97%)
  local copies, waits for them, and re-layouts  9.55 us (3%)
    pallas_call x1, Pallas kernels, whole_lines(): pl.pallas_call(functools.partial(ring_kernel, count, cols, lines), out_sh...  331 us
    unnamed x2, local copies, waits for them, and re-layouts  7.9 us

commit v1 on v0

--- a/solution.py
+++ b/solution.py
@@ -172,8 +172,6 @@
             dressed = jnp.dot(first_order, operator[...], preferred_element_type=jnp.float32).astype(jnp.bfloat16)
             total[rows, :] = (summed + dressed.astype(jnp.float32)) / denominator
 
-        write_line(line).start()
-
     def multiply(item):
         line, within = lax.div(item, group), lax.rem(item, group)
         step, sub = lax.div(within, SUBS), lax.rem(within, SUBS)
@@ -194,10 +192,13 @@
 
         @pl.when(within == group - 1)
         def _():
-            end_line(line)
-
-    @pl.loop(0, events)
-    def _(event):
+            @pl.when(line < lines - 1)
+            def _():
+                end_line(line)
+
+            write_line(line).start()
+
+    def arrive(event):
         line = lax.div(event, group - SUBS)
         slot = event + SUBS * (line + 1)
         last = lax.rem(slot, group) >= group - SUBS
@@ -209,6 +210,8 @@
             def _():
                 hop(way, land.at[way, source], source + SUBS).start()
 
+    @pl.loop(0, events)
+    def _(event):
         @pl.when(event == start * 3 // 4)
         def _():
             for k in range(1, chips):
@@ -223,11 +226,15 @@
                 origin = lax.rem(sibling + cols - 2 * k, cols)
                 w_copy(2 * k, panel.at[origin], origin, sibling).wait_recv()
 
-        @pl.when(event >= start)
-        def _():
-            @pl.loop(0, 2)
-            def _(which):
+        @pl.loop(0, 2)
+        def _(which):
+            @pl.when(event >= start)
+            def _():
                 multiply(2 * (event - start) + which)
+
+            @pl.when(which == 0)
+            def _():
+                arrive(event)
 
     write_line(lines - 1).wait()
 
@@ -242,6 +249,40 @@
         w_copy(2 * k - 1, interaction, col, sibling).wait_send()
         origin = from_chip(k)
         w_copy(2 * k, panel.at[origin], origin, sibling).wait_send()
+
+
+def finish_kernel(mixed, dressing, row_energy, column_energy, out):
+    orbitals = dressing.shape[0]
+    done = out.shape[1] - orbitals
+    if done:
+        out[:, :done] = mixed[:, :done]
+    summed = mixed[:, done:]
+    denominator = row_energy[...] + column_energy[...]
+    first_order = (summed / denominator).astype(jnp.bfloat16)
+    dressed = jnp.dot(first_order, dressing[...], preferred_element_type=jnp.float32).astype(jnp.bfloat16)
+    out[:, done:] = (summed + dressed.astype(jnp.float32)) / denominator
+
+
+def finish_last(mixed, dressing, row_energy, column_energy):
+    rows, columns = mixed.shape
+    orbitals = dressing.shape[0]
+    tile = rows // 8
+    return pl.pallas_call(
+        finish_kernel,
+        out_shape=jax.ShapeDtypeStruct((rows, columns), jnp.float32),
+        grid=(rows // tile,),
+        in_specs=[
+            pl.BlockSpec((tile, columns), lambda i: (i, 0)),
+            pl.BlockSpec((orbitals, orbitals), lambda i: (0, 0)),
+            pl.BlockSpec((tile, 1), lambda i: (i, 0)),
+            pl.BlockSpec((1, orbitals), lambda i: (0, 0)),
+        ],
+        out_specs=pl.BlockSpec((tile, columns), lambda i: (i, 0)),
+        compiler_params=pltpu.CompilerParams(vmem_limit_bytes=60 * 1024 * 1024),
+        cost_estimate=pl.CostEstimate(
+            flops=2 * rows * orbitals * orbitals, bytes_accessed=8 * rows * columns, transcendentals=0
+        ),
+    )(mixed, dressing, row_energy, column_energy)
 
 
 def whole_lines(mesh, interaction, amplitudes, driver, dressing, row_energy, column_energy):
@@ -254,7 +295,9 @@
     dma = pltpu.SemaphoreType.DMA
     anywhere = pl.BlockSpec(memory_space=pl.ANY)
     vmem = pl.BlockSpec(memory_space=pltpu.VMEM)
-    return pl.pallas_call(
+    row_energy = row_energy[:, None]
+    column_energy = column_energy.reshape(lines, orbitals)
+    mixed = pl.pallas_call(
         functools.partial(ring_kernel, count, cols, lines),
         out_shape=jax.ShapeDtypeStruct((rows, columns), jnp.float32),
         in_specs=[anywhere] * 4 + [vmem] * 2,
@@ -278,7 +321,8 @@
         cost_estimate=pl.CostEstimate(
             flops=2 * rows * columns * (depth * count + orbitals), bytes_accessed=2 * rows * columns * 10, transcendentals=0
         ),
-    )(amplitudes, interaction, driver, dressing, row_energy[:, None], column_energy.reshape(lines, orbitals))
+    )(amplitudes, interaction, driver, dressing, row_energy, column_energy)
+    return finish_last(mixed, dressing, row_energy, column_energy[lines - 1 :])
 
 
 def solution(mesh):

time: 341 us -> 342 us (level)
  Pallas kernels: 331 us -> 339 us
  local copies, waits for them, and re-layouts: 9.55 us -> 2.3 us
    pallas_call x0 -> x1, Pallas kernels: none -> 11.5 us  [finish_last(): pl.pallas_call(finish_kernel, out_shape=jax.ShapeDtypeStruct((rows, colum...]
    unnamed x2 -> x1, local copies, waits for them, and re-layouts: 7.9 us -> 0.01 us
    pallas_call x1, Pallas kernels: 331 us -> 327 us  [whole_lines(): pl.pallas_call(functools.partial(ring_kernel, count, cols, lines), out_sh...]
where the time goes in v1:
time: 342 us
  Pallas kernels  339 us (99%)
    pallas_call x1, Pallas kernels, whole_lines(): pl.pallas_call(functools.partial(ring_kernel, count, cols, lines), out_sh...  327 us
    pallas_call x1, Pallas kernels, finish_last(): pl.pallas_call(finish_kernel, out_shape=jax.ShapeDtypeStruct((rows, colum...  11.5 us

profile of v1, /device:TPU:0, one launch (start us, length us, event | category | flops | bytes accessed | tf_op | source)
XLA Modules:
  0.0 341.6 jit_solution(4960313447941042465)
XLA Ops:
  0.0 0.8 subtract_bitcast_fusion
  0.8 0.6 fusion
  1.4 0.6 reshape.8.column_energy
  2.0 1.1 copy.7.row_energy
  3.1 327.0 %shard_map.64.mixed = f32[1024,2048]{1,0:T(8,128)} custom-call(bf16[1024,2048]{1,0:T(8,128)(2,1)} %amplitudes.1, bf16[1024,2048]{1,0:T(8,128)(2,1)} %interaction.1, bf16[1024,2048]{1,0:T(8,128)(2,1)} %driver.1, bf16[1024,1024]{1,0:T(8,128)(2,1)} %dressing.3, f32[1024,1]{1,0:T(8,128)} %copy.7.row_energy, f32[2,1024]{1,0:T(2,128)} %reshape.8.column_energy), custom_call_target="tpu_custom_call" | custom-call | flops 38654705664 | bytes 41943040 | tf_op jit(solution)/shard_map/pallas_call | solution.py:300
  330.1 11.5 %shard_map.65 = f32[1024,2048]{1,0:T(8,128)} custom-call(f32[1024,2048]{1,0:T(8,128)} %shard_map.64.mixed, bf16[1024,1024]{1,0:T(8,128)(2,1)} %dressing.3, f32[1024,1]{1,0:T(8,128)} %copy.7.row_energy, f32[1,1024]{1,0:T(1,128)} %bitcast.10), custom_call_target="tpu_custom_call" | custom-call | flops 2147483648 | bytes 16777216 | tf_op jit(solution)/shard_map/pallas_call | solution.py:270
  (2 shorter events, 0.0 us)

commit v2 on v1

--- a/solution.py
+++ b/solution.py
@@ -73,8 +73,17 @@
 SUBS = 4
 
 
+def energy_sum(occ_energy, vir_energy, first_row, tile, line):
+    orbitals = vir_energy.shape[1]
+    start = pl.multiple_of(lax.rem(first_row, orbitals), tile)
+    across = jnp.broadcast_to(vir_energy[:, pl.ds(start, tile)], (128, tile))
+    row_energy = occ_energy[lax.div(first_row, orbitals)] - across.T[:, :1]
+    column_energy = occ_energy[line] - vir_energy[...]
+    return row_energy + column_energy
+
+
 def ring_kernel(
-    count, cols, lines, amplitudes, interaction, driver, dressing, row_energy, column_energy, out,
+    count, cols, lines, amplitudes, interaction, driver, dressing, occ_energy, vir_energy, out,
     land, panel, total, driver_line, operator, send_sem, recv_sem, w_send, w_recv, own_sem, local_sem,
 ):
     row, col = lax.axis_index("row"), lax.axis_index("col")
@@ -167,7 +176,9 @@
         def _(index):
             rows = pl.ds(pl.multiple_of(index * tile, tile), tile)
             summed = total[rows, :]
-            denominator = row_energy[rows, :] + column_energy[pl.ds(line, 1), :]
+            denominator = energy_sum(
+                occ_energy, vir_energy, row * total.shape[0] + index * tile, tile, col * lines + line
+            )
             first_order = (summed / denominator).astype(jnp.bfloat16)
             dressed = jnp.dot(first_order, operator[...], preferred_element_type=jnp.float32).astype(jnp.bfloat16)
             total[rows, :] = (summed + dressed.astype(jnp.float32)) / denominator
@@ -251,30 +262,33 @@
         w_copy(2 * k, panel.at[origin], origin, sibling).wait_send()
 
 
-def finish_kernel(mixed, dressing, row_energy, column_energy, out):
+def finish_kernel(lines, grid, mixed, dressing, occ_energy, vir_energy, out):
+    tile = mixed.shape[0]
     orbitals = dressing.shape[0]
     done = out.shape[1] - orbitals
     if done:
         out[:, :done] = mixed[:, :done]
     summed = mixed[:, done:]
-    denominator = row_energy[...] + column_energy[...]
+    first_row = (lax.axis_index("row") * grid + pl.program_id(0)) * tile
+    line = lax.axis_index("col") * lines + lines - 1
+    denominator = energy_sum(occ_energy, vir_energy, first_row, tile, line)
     first_order = (summed / denominator).astype(jnp.bfloat16)
     dressed = jnp.dot(first_order, dressing[...], preferred_element_type=jnp.float32).astype(jnp.bfloat16)
     out[:, done:] = (summed + dressed.astype(jnp.float32)) / denominator
 
 
-def finish_last(mixed, dressing, row_energy, column_energy):
+def finish_last(mixed, dressing, occ_energy, vir_energy):
     rows, columns = mixed.shape
     orbitals = dressing.shape[0]
-    tile = rows // 8
+    tile = rows // 4
     return pl.pallas_call(
-        finish_kernel,
+        functools.partial(finish_kernel, columns // orbitals, rows // tile),
         out_shape=jax.ShapeDtypeStruct((rows, columns), jnp.float32),
         grid=(rows // tile,),
         in_specs=[
             pl.BlockSpec((tile, columns), lambda i: (i, 0)),
             pl.BlockSpec((orbitals, orbitals), lambda i: (0, 0)),
-            pl.BlockSpec((tile, 1), lambda i: (i, 0)),
+            pl.BlockSpec(memory_space=pltpu.SMEM),
             pl.BlockSpec((1, orbitals), lambda i: (0, 0)),
         ],
         out_specs=pl.BlockSpec((tile, columns), lambda i: (i, 0)),
@@ -282,10 +296,10 @@
         cost_estimate=pl.CostEstimate(
             flops=2 * rows * orbitals * orbitals, bytes_accessed=8 * rows * columns, transcendentals=0
         ),
-    )(mixed, dressing, row_energy, column_energy)
-
-
-def whole_lines(mesh, interaction, amplitudes, driver, dressing, row_energy, column_energy):
+    )(mixed, dressing, occ_energy, vir_energy)
+
+
+def whole_lines(mesh, interaction, amplitudes, driver, dressing, occ_energy, vir_energy):
     count, cols = mesh.shape["row"], mesh.shape["col"]
     rows, columns = driver.shape
     depth = amplitudes.shape[0]
@@ -295,12 +309,11 @@
     dma = pltpu.SemaphoreType.DMA
     anywhere = pl.BlockSpec(memory_space=pl.ANY)
     vmem = pl.BlockSpec(memory_space=pltpu.VMEM)
-    row_energy = row_energy[:, None]
-    column_energy = column_energy.reshape(lines, orbitals)
+    vir_energy = vir_energy[None, :]
     mixed = pl.pallas_call(
         functools.partial(ring_kernel, count, cols, lines),
         out_shape=jax.ShapeDtypeStruct((rows, columns), jnp.float32),
-        in_specs=[anywhere] * 4 + [vmem] * 2,
+        in_specs=[anywhere] * 4 + [pl.BlockSpec(memory_space=pltpu.SMEM), vmem],
         out_specs=anywhere,
         scratch_shapes=[
             pltpu.VMEM((2, slots, depth // 2, orbitals // SUBS), jnp.bfloat16),
@@ -321,8 +334,8 @@
         cost_estimate=pl.CostEstimate(
             flops=2 * rows * columns * (depth * count + orbitals), bytes_accessed=2 * rows * columns * 10, transcendentals=0
         ),
-    )(amplitudes, interaction, driver, dressing, row_energy, column_energy)
-    return finish_last(mixed, dressing, row_energy, column_energy[lines - 1 :])
+    )(amplitudes, interaction, driver, dressing, occ_energy, vir_energy)
+    return finish_last(mixed, dressing, occ_energy, vir_energy)
 
 
 def solution(mesh):
@@ -333,7 +346,7 @@
         row_energy = line_energy(occ_energy, vir_energy, lax.axis_index("row") * row_count, row_count)
         column_energy = line_energy(occ_energy, vir_energy, lax.axis_index("col") * column_count, column_count)
         if column_count % dressing.shape[0] == 0:
-            return whole_lines(mesh, interaction, amplitudes, driver, dressing, row_energy, column_energy)
+            return whole_lines(mesh, interaction, amplitudes, driver, dressing, occ_energy, vir_energy)
         cycle_term = cycle(interaction, amplitudes, count)
         denominator = row_energy[:, None] + column_energy[None, :]
         summed = driver.astype(jnp.float32) + cycle_term

time: 342 us -> 336 us (0.982)
  no operation moved by 1% of the time
where the time goes in v2:
time: 336 us
  Pallas kernels  336 us (100%)
    pallas_call x1, Pallas kernels, whole_lines(): pl.pallas_call(functools.partial(ring_kernel, count, cols, lines), out_sh...  327 us
    pallas_call x1, Pallas kernels, finish_last(): pl.pallas_call(functools.partial(finish_kernel, columns // orbitals, rows...  9.72 us

profile of v2, /device:TPU:0, one launch (start us, length us, event | category | flops | bytes accessed | tf_op | source)
XLA Modules:
  0.0 336.3 jit_solution(13382489240186178742)
XLA Ops:
  0.0 326.6 %shard_map.64.mixed = f32[1024,2048]{1,0:T(8,128)} custom-call(bf16[1024,2048]{1,0:T(8,128)(2,1)} %amplitudes.1, bf16[1024,2048]{1,0:T(8,128)(2,1)} %interaction.1, bf16[1024,2048]{1,0:T(8,128)(2,1)} %driver.1, bf16[1024,1024]{1,0:T(8,128)(2,1)} %dressing.3, f32[8]{0:T(128)} %occ_energy.3, f32[1,1024]{1,0:T(1,128)} %bitcast.1), custom_call_target="tpu_custom_call" | custom-call | flops 38654705664 | bytes 41943040 | tf_op jit(solution)/shard_map/pallas_call | solution.py:313
  326.6 9.7 %shard_map.65 = f32[1024,2048]{1,0:T(8,128)} custom-call(f32[1024,2048]{1,0:T(8,128)} %shard_map.64.mixed, bf16[1024,1024]{1,0:T(8,128)(2,1)} %dressing.3, f32[8]{0:T(128)} %occ_energy.3, f32[1,1024]{1,0:T(1,128)} %bitcast.2), custom_call_target="tpu_custom_call" | custom-call | flops 2147483648 | bytes 16777216 | tf_op jit(solution)/shard_map/pallas_call | solution.py:284
